TPU v7x, 256 devices: a whole 4x4x8 slice. The times are simulated.
256 devices in a mesh: tm: 8 (over z), atom: 2 (over x_lo), chan: 16 (over y, x_hi, core).
Axes of the slice: x: 4 (x_hi: 2, x_lo: 2; x = x_hi * 2 + x_lo), y: 4, z: 8, core: 2. Of those that a mesh axis runs over, the one named last changes fastest.
Arguments:
- signal: bfloat16 [256, 8192], P('chan', 'tm'), may hold values from -6 to 6
- codes_init: float32 [128, 8192], P('atom', 'tm'), may hold values from -4 to 4
- atom_bank: bfloat16 [128, 256, 512], P('atom', 'chan'), may hold values from -0.015625 to 0.015625
- step_size: float32 [128], P('atom'), may hold values from 0.1 to 0.5
- threshold: float32 [128], P('atom'), may hold values from 0.3 to 3
Outputs:
- final_codes: float32 [128, 8192], P('atom', 'tm')
- residual: float32 [256, 8192], P('chan', 'tm')
All inputs are finite; a program needn't handle non-finite values.
Results may differ from a plain program's by a relative error of at most 0.0025.
Values may be sent and summed in bfloat16 or wider, within the bound.
A program may use at most 64 MiB of HBM per device.

v0:
```python
import jax
import jax.numpy as jnp
from jax import lax
from jax.sharding import PartitionSpec as P

ITERS = 2


def from_behind(value, axis, steps):
    count = lax.axis_size(axis)
    leading, last = (max(0, -steps), min(count, count - steps))
    return lax.ppermute(value, axis, [(source, source + steps) for source in range(leading, last)])


def synthesize(extended, atom_bank):
    atom_rows, chan_rows, taps = atom_bank.shape
    group = min(32, taps)
    turns = taps // group
    length = extended.shape[1] - taps + 1
    weights = (
        atom_bank.reshape(atom_rows, chan_rows, turns, group)
        .transpose(2, 1, 3, 0)
        .reshape(turns, chan_rows, group * atom_rows)
    )

    def synthesize_accumulate(turn_index, total):
        start = taps - group - turn_index * group
        window = lax.dynamic_slice_in_dim(extended, start, length + group - 1, 1)
        stacked = jnp.concatenate(
            [
                window[:, group - 1 - offset : group - 1 - offset + length]
                for offset in range(group)
            ],
            axis=0,
        )
        return total + jnp.dot(weights[turn_index], stacked, preferred_element_type=jnp.float32)

    return lax.fori_loop(
        0, turns, synthesize_accumulate, jnp.zeros((chan_rows, length), jnp.float32)
    )


def correlate(extended, atom_bank):
    atom_rows, chan_rows, taps = atom_bank.shape
    group = min(32, taps)
    turns = taps // group
    length = extended.shape[1] - taps + 1
    weights = (
        atom_bank.reshape(atom_rows, chan_rows, turns, group)
        .transpose(2, 0, 3, 1)
        .reshape(turns, atom_rows, group * chan_rows)
    )

    def correlate_accumulate(turn_index, total):
        start = turn_index * group
        window = lax.dynamic_slice_in_dim(extended, start, length + group - 1, 1)
        stacked = jnp.concatenate(
            [window[:, offset : offset + length] for offset in range(group)], axis=0
        )
        return total + jnp.dot(weights[turn_index], stacked, preferred_element_type=jnp.float32)

    return lax.fori_loop(
        0, turns, correlate_accumulate, jnp.zeros((atom_rows, length), jnp.float32)
    )


def shrink(current, gradient, step_size, threshold):
    moved = current - step_size[:, None] * gradient
    bound = (step_size * threshold)[:, None]
    return moved - jnp.clip(moved, -bound, bound)


def body(signal, codes_init, atom_bank, step_size, threshold):
    taps = atom_bank.shape[2]
    slab = signal.shape[1]
    current = codes_init
    misfit = None
    for sweep_index in range(ITERS):
        lowered = current.astype(jnp.bfloat16)
        earlier = from_behind(lowered[:, slab - taps + 1 :], "tm", 1)
        partial_recon = synthesize(jnp.concatenate([earlier, lowered], axis=1), atom_bank)
        recon = lax.psum(partial_recon, "atom")
        misfit = recon - signal.astype(jnp.float32)
        rounded = misfit.astype(jnp.bfloat16)
        following = from_behind(rounded[:, : taps - 1], "tm", -1)
        partial_grad = correlate(jnp.concatenate([rounded, following], axis=1), atom_bank)
        gradient = lax.psum(partial_grad, "chan")
        current = shrink(current, gradient, step_size, threshold)
    return (current, misfit)


def solution(mesh):
    placed = (P("chan", "tm"), P("atom", "tm"), P("atom", "chan", None), P("atom"), P("atom"))
    return jax.shard_map(
        body,
        mesh=mesh,
        in_specs=placed,
        out_specs=(P("atom", "tm"), P("chan", "tm")),
        check_vma=False,
    )
```

profile of v0, /device:TPU:1, one launch (start us, length us, event | category | flops | bytes accessed | tf_op | source)
XLA Modules:
  0.0 1402.1 jit_solution(5570843952976790271)
XLA Ops:
  8.3 4.4 collective-permute-start
  18.4 435.2 %while.60 = (s32[]{:T(128)}, f32[16,1024]{1,0:T(8,128)S(1)}, bf16[16,16,2048]{2,1,0:T(8,128)(2,1)}, bf16[64,1535]{1,0:T(8,128)(2,1)S(1)}, s32[]{:T(128)}, /*inde...) while((s32[]{:T(128)}, f32[16,1024]{1,0:T(8,128)S(1)}, ...), condition=%wide.region_1.0_spmd.clone, body=%wide.region_0.0_spmd.clone.sunk | while | flops 67141672 | bytes 12780941 | solution.py:38
  454.3 34.5 %all-reduce.5.cloned.1.call-done = f32[16,1024]{1,0:T(8,128)} async-done(((f32[16,1024]{1,0:T(8,128)}), f32[16,1024]{1,0:T(8,128)}) %all-reduce.5.cloned.1.call-update) | async-done | bytes 65552 | tf_op jit(solution)/shard_map/psum | solution.py:82
  495.4 61.8 %while.61 = (s32[]{:T(128)}, f32[64,1024]{1,0:T(8,128)S(1)}, bf16[16,64,512]{2,1,0:T(8,128)(2,1)}, bf16[16,1535]{1,0:T(8,128)(2,1)S(1)}, s32[]{:T(128)}, /*index...) while((s32[]{:T(128)}, f32[64,1024]{1,0:T(8,128)S(1)}, ...), condition=%wide.region_4.0_spmd.clone, body=%wide.region_3.0_spmd.clone.sunk | while | flops 67239976 | bytes 3736953 | solution.py:62
  558.0 145.2 %all-reduce.7.cloned.1.call-done = f32[64,1024]{1,0:T(8,128)} async-done(((f32[64,1024]{1,0:T(8,128)}), f32[64,1024]{1,0:T(8,128)}) %all-reduce.7.cloned.1.call-update) | async-done | bytes 262160 | tf_op jit(solution)/shard_map/psum | solution.py:87
  704.4 3.4 collective-permute-start.2
  709.0 435.2 %while.62 = (s32[]{:T(128)}, f32[16,1024]{1,0:T(8,128)S(1)}, bf16[16,16,2048]{2,1,0:T(8,128)(2,1)}, bf16[64,1535]{1,0:T(8,128)(2,1)S(1)}, s32[]{:T(128)}, /*inde...) while((s32[]{:T(128)}, f32[16,1024]{1,0:T(8,128)S(1)}, ...), condition=%wide.region_7.8_spmd.clone, body=%wide.region_6.7_spmd.clone.sunk | while | flops 67141672 | bytes 12780941 | solution.py:38
  733.4 2.9 convolution_add_fusion.10
  760.6 2.9 convolution_add_fusion.10
  787.8 2.9 convolution_add_fusion.10
  815.0 2.9 convolution_add_fusion.10
  842.2 2.9 convolution_add_fusion.10
  869.4 2.9 convolution_add_fusion.10
  896.6 2.9 convolution_add_fusion.10
  923.8 2.9 convolution_add_fusion.10
  951.0 2.9 convolution_add_fusion.10
  978.2 2.9 convolution_add_fusion.10
  1005.4 2.9 convolution_add_fusion.10
  1032.6 2.9 convolution_add_fusion.10
  1059.8 2.9 convolution_add_fusion.10
  1145.0 35.0 %all-reduce.9.cloned.1.call-done = f32[16,1024]{1,0:T(8,128)} async-done(((f32[16,1024]{1,0:T(8,128)}), f32[16,1024]{1,0:T(8,128)}) %all-reduce.9.cloned.1.call-update) | async-done | bytes 65552 | tf_op jit(solution)/shard_map/psum | solution.py:82
  1182.8 3.2 collective-permute-done.3
  1186.0 61.8 %while.63 = (s32[]{:T(128)}, f32[64,1024]{1,0:T(8,128)S(1)}, bf16[16,64,512]{2,1,0:T(8,128)(2,1)}, bf16[16,1535]{1,0:T(8,128)(2,1)S(1)}, s32[]{:T(128)}, /*index...) while((s32[]{:T(128)}, f32[64,1024]{1,0:T(8,128)S(1)}, ...), condition=%wide.region_10.11_spmd.clone, body=%wide.region_9.10_spmd.clone.sunk | while | flops 67239976 | bytes 3736953 | solution.py:62
  1248.5 145.2 %all-reduce.11.cloned.1.call-done = f32[64,1024]{1,0:T(8,128)} async-done(((f32[64,1024]{1,0:T(8,128)}), f32[64,1024]{1,0:T(8,128)}) %all-reduce.11.cloned.1.call-update) | async-done | bytes 262160 | tf_op jit(solution)/shard_map/psum | solution.py:87
  (2155 shorter events, 977.7 us)
Async XLA Ops:
  7.2 481.7 %all-reduce.5.cloned.1.call-start = ((), (), s32[]{:S(2)}) async-start(), calls=%async_computation | async-start | bytes 131072 | tf_op jit(solution)/shard_map/psum | solution.py:82
  8.3 10.0 collective-permute-start
  18.4 470.5 %copy-start.7 = (bf16[16,1024]{1,0:T(8,128)(2,1)S(1)}, bf16[16,1024]{1,0:T(8,128)(2,1)}, u32[]{:S(2)}) copy-start(bf16[16,1024]{1,0:T(8,128)(2,1)} %param.13) | copy-start | bytes 98308
  18.4 472.6 %copy-start.2 = (bf16[64,16,512]{2,1,0:T(8,128)(2,1)S(1)}, bf16[64,16,512]{2,1,0:T(8,128)(2,1)}, u32[]{:S(2)}) copy-start(bf16[64,16,512]{2,1,0:T(8,128)(2,1)} %param.15) | copy-start | bytes 3145732
  453.6 0.6 copy-start.3
  454.3 249.0 %all-reduce.7.cloned.1.call-start = ((), (), s32[]{:S(2)}) async-start(), calls=%async_computation.1 | async-start | bytes 524288 | tf_op jit(solution)/shard_map/psum | solution.py:87
  489.7 5.6 collective-permute-start.1
  495.3 62.7 %copy-start.8 = (f32[64]{0:T(128)S(1)}, f32[64]{0:T(128)}, u32[]{:S(2)}) copy-start(f32[64]{0:T(128)} %param.16) | copy-start | bytes 772
  495.3 62.7 %copy-start.9 = (f32[64]{0:T(128)S(1)}, f32[64]{0:T(128)}, u32[]{:S(2)}) copy-start(f32[64]{0:T(128)} %param.17) | copy-start | bytes 772
  495.3 207.9 %copy-start.5 = (f32[64,1024]{1,0:T(8,128)S(1)}, f32[64,1024]{1,0:T(8,128)}, u32[]{:S(2)}) copy-start(f32[64,1024]{1,0:T(8,128)} %param.14) | copy-start | bytes 786436
  557.2 0.7 copy-start
  557.9 622.0 %all-reduce.9.cloned.1.call-start = ((), (), s32[]{:S(2)}) async-start(), calls=%async_computation.2 | async-start | bytes 131072 | tf_op jit(solution)/shard_map/psum | solution.py:82
  704.4 4.5 collective-permute-start.2
  1144.2 0.6 copy-start.4
  1144.9 248.8 %all-reduce.11.cloned.1.call-start = ((), (), s32[]{:S(2)}) async-start(), calls=%async_computation.3 | async-start | bytes 524288 | tf_op jit(solution)/shard_map/psum | solution.py:87
  1181.5 4.5 collective-permute-start.3
  1185.9 207.8 %copy-start.6 = (f32[64,1024]{1,0:T(8,128)S(1)}, f32[64,1024]{1,0:T(8,128)}, u32[]{:S(2)}) copy-start(f32[64,1024]{1,0:T(8,128)} %all-reduce.7.cloned.1.call-done) | copy-start | bytes 786436
  1247.8 0.7 copy-start.1
Sparse Core Ops, SparseCore 0:
  454.4 34.3 all-reduce.4
  558.1 145.1 all-reduce.6
  1145.0 34.9 all-reduce.8
  1248.7 145.0 all-reduce.10
where the time goes:
time: 1400 us
  local copies, waits for them, and re-layouts  876 us (63%)
  waiting for transfers between devices  364 us (26%)
  matrix products  129 us (9%)
  between operations  14 us (1%)
    while x1984, local copies, waits for them, and re-layouts  836 us
    psum x2, waiting for transfers between devices, body(): gradient = lax.psum(partial_grad, 'chan')  290 us
    dot_general x32, matrix products, synthesize_accumulate(): jnp.dot(weights[turn_index], stacked, preferred_element_type=jnp.float32)  92.1 us
    psum x2, waiting for transfers between devices, body(): recon = lax.psum(partial_recon, 'atom')  69.5 us
    dot_general x32, matrix products, correlate_accumulate(): jnp.dot(weights[turn_index], stacked, preferred_element_type=jnp.float32)  37 us
  transfers between devices with their start and end apart: 8, of which 6 were waited for; matrix products, arithmetic and copies ran while one was open for 1% of the time, Pallas kernels for 0%

commit v1 on v0

--- a/solution.py
+++ b/solution.py
@@ -84,7 +84,7 @@
         rounded = misfit.astype(jnp.bfloat16)
         following = from_behind(rounded[:, : taps - 1], "tm", -1)
         partial_grad = correlate(jnp.concatenate([rounded, following], axis=1), atom_bank)
-        gradient = lax.psum(partial_grad, "chan")
+        gradient = jnp.sum(lax.all_gather(partial_grad, "chan"), axis=0)
         current = shrink(current, gradient, step_size, threshold)
     return (current, misfit)
 

time: 1400 us -> 1240 us (0.89)
  waiting for transfers between devices: 364 us -> 198 us
    psum x2 -> x0, waiting for transfers between devices: 290 us -> none  [body(): gradient = lax.psum(partial_grad, 'chan')]
    all_gather x0 -> x2, waiting for transfers between devices: none -> 127 us  [body(): gradient = jnp.sum(lax.all_gather(partial_grad, 'chan'), axis=0)]
where the time goes in v1:
time: 1240 us
  local copies, waits for them, and re-layouts  872 us (70%)
  waiting for transfers between devices  198 us (16%)
  matrix products  129 us (10%)
  between operations  14 us (1%)
    while x1984, local copies, waits for them, and re-layouts  832 us
    all_gather x2, waiting for transfers between devices, body(): gradient = jnp.sum(lax.all_gather(partial_grad, 'chan'), axis=0)  127 us
    dot_general x32, matrix products, synthesize_accumulate(): jnp.dot(weights[turn_index], stacked, preferred_element_type=jnp.float32)  92.1 us
    psum x2, waiting for transfers between devices, body(): recon = lax.psum(partial_recon, 'atom')  67 us
    dot_general x32, matrix products, correlate_accumulate(): jnp.dot(weights[turn_index], stacked, preferred_element_type=jnp.float32)  37 us
  transfers between devices with their start and end apart: 8, of which 6 were waited for; matrix products, arithmetic and copies ran while one was open for 1% of the time, Pallas kernels for 0%

profile of v1, /device:TPU:1, one launch (start us, length us, event | category | flops | bytes accessed | tf_op | source)
XLA Modules:
  0.0 1235.2 jit_solution(4469470745625312910)
XLA Ops:
  8.3 4.4 collective-permute-start
  18.4 433.3 %while.60 = (s32[]{:T(128)}, f32[16,1024]{1,0:T(8,128)S(1)}, bf16[16,16,2048]{2,1,0:T(8,128)(2,1)}, bf16[64,1535]{1,0:T(8,128)(2,1)S(1)}, s32[]{:T(128)}, /*inde...) while((s32[]{:T(128)}, f32[16,1024]{1,0:T(8,128)S(1)}, ...), condition=%wide.region_1.0_spmd.clone, body=%wide.region_0.0_spmd.clone.sunk | while | flops 67141672 | bytes 12780941 | solution.py:38
  69.7 2.9 convolution_add_fusion.8
  96.8 2.9 convolution_add_fusion.8
  150.9 2.9 convolution_add_fusion.8
  178.0 2.9 convolution_add_fusion.8
  232.2 2.9 convolution_add_fusion.8
  286.3 2.9 convolution_add_fusion.8
  313.4 2.9 convolution_add_fusion.8
  367.5 2.9 convolution_add_fusion.8
  394.6 2.9 convolution_add_fusion.8
  448.8 2.9 convolution_add_fusion.8
  452.4 34.5 %all-reduce.3.cloned.1.call-done = f32[16,1024]{1,0:T(8,128)} async-done(((f32[16,1024]{1,0:T(8,128)}), f32[16,1024]{1,0:T(8,128)}) %all-reduce.3.cloned.1.call-update) | async-done | bytes 65552 | tf_op jit(solution)/shard_map/psum | solution.py:82
  493.4 61.8 %while.61 = (s32[]{:T(128)}, f32[64,1024]{1,0:T(8,128)S(1)}, bf16[16,64,512]{2,1,0:T(8,128)(2,1)}, bf16[16,1535]{1,0:T(8,128)(2,1)S(1)}, s32[]{:T(128)}, /*index...) while((s32[]{:T(128)}, f32[64,1024]{1,0:T(8,128)S(1)}, ...), condition=%wide.region_4.0_spmd.clone, body=%wide.region_3.0_spmd.clone.sunk | while | flops 67239976 | bytes 3736953 | solution.py:62
  556.1 63.4 %all-gather.5.cloned.1.call-done = f32[1024,1024]{1,0:T(8,128)} async-done(((f32[64,1024]{1,0:T(8,128)}), f32[1024,1024]{1,0:T(8,128)}) %all-gather.5.cloned.1.call-update) | async-done | bytes 4194320 | tf_op jit(solution)/shard_map/all_gather | solution.py:87
  622.2 3.4 collective-permute-start.2
  626.8 433.3 %while.62 = (s32[]{:T(128)}, f32[16,1024]{1,0:T(8,128)S(1)}, bf16[16,16,2048]{2,1,0:T(8,128)(2,1)}, bf16[64,1535]{1,0:T(8,128)(2,1)S(1)}, s32[]{:T(128)}, /*inde...) while((s32[]{:T(128)}, f32[16,1024]{1,0:T(8,128)S(1)}, ...), condition=%wide.region_7.8_spmd.clone, body=%wide.region_6.7_spmd.clone.sunk | while | flops 67141672 | bytes 12780941 | solution.py:38
  678.1 2.9 convolution_add_fusion.10
  705.2 2.9 convolution_add_fusion.10
  759.3 2.9 convolution_add_fusion.10
  1060.8 32.5 %all-reduce.5.cloned.1.call-done = f32[16,1024]{1,0:T(8,128)} async-done(((f32[16,1024]{1,0:T(8,128)}), f32[16,1024]{1,0:T(8,128)}) %all-reduce.5.cloned.1.call-update) | async-done | bytes 65552 | tf_op jit(solution)/shard_map/psum | solution.py:82
  1096.1 3.2 collective-permute-done.3
  1099.3 61.8 %while.63 = (s32[]{:T(128)}, f32[64,1024]{1,0:T(8,128)S(1)}, bf16[16,64,512]{2,1,0:T(8,128)(2,1)}, bf16[16,1535]{1,0:T(8,128)(2,1)S(1)}, s32[]{:T(128)}, /*index...) while((s32[]{:T(128)}, f32[64,1024]{1,0:T(8,128)S(1)}, ...), condition=%wide.region_10.11_spmd.clone, body=%wide.region_9.10_spmd.clone.sunk | while | flops 67239976 | bytes 3736953 | solution.py:62
  1161.9 63.5 %all-gather.7.cloned.1.call-done = f32[1024,1024]{1,0:T(8,128)} async-done(((f32[64,1024]{1,0:T(8,128)}), f32[1024,1024]{1,0:T(8,128)}) %all-gather.7.cloned.1.call-update) | async-done | bytes 4194320 | tf_op jit(solution)/shard_map/all_gather | solution.py:87
  (2155 shorter events, 976.9 us)
Async XLA Ops:
  7.2 479.7 %all-reduce.3.cloned.1.call-start = ((), (), s32[]{:S(2)}) async-start(), calls=%async_computation | async-start | bytes 131072 | tf_op jit(solution)/shard_map/psum | solution.py:82
  8.3 10.0 collective-permute-start
  18.4 468.5 %copy-start.6 = (bf16[16,1024]{1,0:T(8,128)(2,1)S(1)}, bf16[16,1024]{1,0:T(8,128)(2,1)}, u32[]{:S(2)}) copy-start(bf16[16,1024]{1,0:T(8,128)(2,1)} %param.13) | copy-start | bytes 98308
  18.4 470.7 %copy-start.2 = (bf16[64,16,512]{2,1,0:T(8,128)(2,1)S(1)}, bf16[64,16,512]{2,1,0:T(8,128)(2,1)}, u32[]{:S(2)}) copy-start(bf16[64,16,512]{2,1,0:T(8,128)(2,1)} %param.15) | copy-start | bytes 3145732
  451.7 0.6 copy-start.3
  452.3 167.2 %all-gather.5.cloned.1.call-start = ((), (), s32[]{:S(2)}) async-start(), calls=%async_computation.2 | async-start | bytes 4456448 | tf_op jit(solution)/shard_map/all_gather | solution.py:87
  487.7 5.6 collective-permute-start.1
  493.4 62.7 %copy-start.7 = (f32[64]{0:T(128)S(1)}, f32[64]{0:T(128)}, u32[]{:S(2)}) copy-start(f32[64]{0:T(128)} %param.16) | copy-start | bytes 772
  493.4 62.7 %copy-start.8 = (f32[64]{0:T(128)S(1)}, f32[64]{0:T(128)}, u32[]{:S(2)}) copy-start(f32[64]{0:T(128)} %param.17) | copy-start | bytes 772
  555.2 0.7 copy-start
  555.3 66.7 %copy-start.5 = (f32[64,1024]{1,0:T(8,128)S(1)}, f32[64,1024]{1,0:T(8,128)}, u32[]{:S(2)}) copy-start(f32[64,1024]{1,0:T(8,128)} %param.14) | copy-start | bytes 786436
  556.0 537.3 %all-reduce.5.cloned.1.call-start = ((), (), s32[]{:S(2)}) async-start(), calls=%async_computation.1 | async-start | bytes 131072 | tf_op jit(solution)/shard_map/psum | solution.py:82
  622.2 4.5 collective-permute-start.2
  1060.1 0.6 copy-start.4
  1060.8 164.6 %all-gather.7.cloned.1.call-start = ((), (), s32[]{:S(2)}) async-start(), calls=%async_computation.3 | async-start | bytes 4456448 | tf_op jit(solution)/shard_map/all_gather | solution.py:87
  1094.8 4.5 collective-permute-start.3
  1161.1 0.7 copy-start.1
Sparse Core Ops, SparseCore 0:
  452.4 34.3 all-reduce.2
  556.1 63.3 all-gather.4
  1060.9 32.4 all-reduce.4
  1162.0 63.2 all-gather.6
